TPU v7x, 32 devices: a whole 2x2x4 slice. The times are simulated.
32 devices in a mesh: seq: 32 (over z, y, x, core), batch: 1.
Axes of the slice: x: 2, y: 2, z: 4, core: 2. Of those that a mesh axis runs over, the one named last changes fastest.
Arguments:
- tokens: bfloat16 [1, 131072, 1024], P('batch', 'seq'), may hold values from -6 to 6
- cotangent: bfloat16 [1, 131072, 1024], P('batch', 'seq'), may hold values from -6 to 6
- left_factor: bfloat16 [512, 256, 256], P('seq'), may hold values from -0.375 to 0.375
- right_factor: bfloat16 [256, 512, 512], P('seq'), may hold values from -0.25 to 0.25
Outputs:
- output: bfloat16 [1, 131072, 1024], P('batch', 'seq')
- tokens_grad: bfloat16 [1, 131072, 1024], P('batch', 'seq')
- left_grad: float32 [512, 256, 256], P('seq', 'batch')
- right_grad: float32 [256, 512, 512], P('seq', 'batch')
All inputs are finite; a program needn't handle non-finite values.
Results may differ from a plain program's by a relative error of at most 0.0058.
Values may be sent and summed in bfloat16 or wider, within the bound.
A program may use at most 192 MiB of HBM per device.

v0:
```python
import jax
import jax.numpy as jnp
from jax import lax
from jax.sharding import PartitionSpec as P

grad_unscale = 1.0 / 32.0


def shards(tokens, cotangent, left_factor, right_factor):
    a_rows = left_factor.shape[0]
    block_len = left_factor.shape[1]
    channels = tokens.shape[2]
    blocks = tokens.reshape(a_rows, block_len, channels)
    upstream = cotangent.reshape(a_rows, block_len, channels).astype(jnp.float32)
    tokens_f = blocks.astype(jnp.float32)
    gate_sig = jax.nn.sigmoid(tokens_f)
    silu_x = tokens_f * gate_sig
    first = jnp.einsum(
        "apq,aqd->apd", left_factor, blocks, preferred_element_type=jnp.float32
    ).astype(jnp.bfloat16)
    grad_second = (upstream * silu_x).astype(jnp.bfloat16)
    first_cols = lax.all_to_all(first, "seq", split_axis=1, concat_axis=0, tiled=True)
    first_cols, second = (
        first_cols,
        lax.all_to_all(
            jnp.einsum(
                "bij,jbd->ibd", right_factor, first_cols, preferred_element_type=jnp.float32
            ).astype(jnp.bfloat16),
            "seq",
            split_axis=0,
            concat_axis=1,
            tiled=True,
        ),
    )
    grad_cols = lax.all_to_all(grad_second, "seq", split_axis=1, concat_axis=0, tiled=True)
    grad_cols, grad_first = (
        grad_cols,
        lax.all_to_all(
            jnp.einsum(
                "bij,ibd->jbd", right_factor, grad_cols, preferred_element_type=jnp.float32
            ).astype(jnp.bfloat16),
            "seq",
            split_axis=0,
            concat_axis=1,
            tiled=True,
        ),
    )
    right_term = jnp.einsum(
        "ibd,jbd->bij", grad_cols, first_cols, preferred_element_type=jnp.float32
    )
    right_grad = (
        lax.psum_scatter(right_term, "batch", scatter_dimension=1, tiled=True) * grad_unscale
    )
    second_f = second.astype(jnp.float32)
    output = (second_f * silu_x).astype(jnp.bfloat16)
    gate_grad = upstream * second_f * gate_sig * (1.0 + tokens_f * (1.0 - gate_sig))
    tokens_grad = (
        jnp.einsum("apq,apd->aqd", left_factor, grad_first, preferred_element_type=jnp.float32)
        + gate_grad
    ).astype(jnp.bfloat16)
    left_term = jnp.einsum("apd,aqd->apq", grad_first, blocks, preferred_element_type=jnp.float32)
    left_grad = lax.psum_scatter(left_term, "batch", scatter_dimension=1, tiled=True) * grad_unscale
    return (output.reshape(tokens.shape), tokens_grad.reshape(tokens.shape), left_grad, right_grad)


def solution(mesh):
    return jax.shard_map(
        shards,
        mesh=mesh,
        in_specs=(
            P("batch", "seq", None),
            P("batch", "seq", None),
            P("seq", None, None),
            P("seq", None, None),
        ),
        out_specs=(
            P("batch", "seq", None),
            P("batch", "seq", None),
            P("seq", "batch", None),
            P("seq", "batch", None),
        ),
        check_vma=False,
    )
```

profile of v0, /device:TPU:0, one launch (start us, length us, event | category | flops | bytes accessed | tf_op | source)
XLA Modules:
  0.0 832.5 jit_solution(7080597714208468269)
XLA Ops:
  2.2 9.1 %convolution_convert_fusion = bf16[16,256,1024]{2,1,0:T(8,128)(2,1)} fusion(bf16[16,256,256]{2,1,0:T(8,128)(2,1)S(1)} %copy-done, bf16[16,256,1024]{2,1,0:T(8,128)(2,1)} %bitcast.42), kind=kOutput, calls=%fused_computation.36 | convolution fusion | flops 2151677952 | bytes 18874368 | tf_op jit(solution)/shard_map/apq,aqd->apd/dot_general | solution.py:18
  11.4 11.5 %copy.51 = bf16[16,256,1024]{2,0,1:T(8,128)(2,1)} copy(bf16[16,256,1024]{2,1,0:T(8,128)(2,1)} %convolution_convert_fusion) | data formatting | bytes 16777216 | tf_op jit(solution)/shard_map/convert_element_type | solution.py:20
  22.8 8.0 all-to-all-start
  30.8 11.4 %fusion.4 = bf16[16,256,1024]{2,1,0:T(8,128)(2,1)} fusion(bf16[16,256,1024]{2,1,0:T(8,128)(2,1)} %bitcast.47, bf16[16,256,1024]{2,1,0:T(8,128)(2,1)} %bitcast.43), kind=kLoop, calls=%fused_computation.11 | loop fusion | flops 33554432 | bytes 25165824 | tf_op jit(solution)/shard_map/convert_element_type | solution.py:21
  42.2 11.3 %copy.57 = bf16[16,256,1024]{2,0,1:T(8,128)(2,1)} copy(bf16[16,256,1024]{2,1,0:T(8,128)(2,1)} %fusion.4) | data formatting | bytes 16777216 | tf_op jit(solution)/shard_map/convert_element_type | solution.py:21
  53.5 163.4 %all-to-all-done = bf16[16,256,1024]{2,0,1:T(8,128)(2,1)} async-done(((bf16[16,256,1024]{2,0,1:T(8,128)(2,1)}), bf16[16,256,1024]{2,0,1:T(8,128)(2,1)}, u32[]{:S(2)}, u32[]{:S(2)}) %all-to-all-start) | async-done | bytes 8388640 | tf_op jit(solution)/shard_map/all_to_all | solution.py:22
  216.8 3.9 all-to-all-start.2
  220.7 16.0 %copy.53 = bf16[32,16,8,1024]{3,2,1,0:T(8,128)(2,1)} copy(bf16[32,16,8,1024]{3,1,2,0:T(8,128)(2,1)} %bitcast.3) | data formatting | bytes 16777216 | tf_op jit(solution)/shard_map/all_to_all | solution.py:22
  236.7 31.2 %convert_bitcast_fusion.2 = bf16[512,8,1024]{0,2,1:T(8,128)(2,1)} fusion(bf16[8,512,512]{2,1,0:T(8,128)(2,1)S(1)} %copy-done.1, bf16[512,8,1024]{2,1,0:T(8,128)(2,1)} %bitcast.49), kind=kOutput, calls=%fused_computation.26 | convolution fusion | flops 4299161600 | bytes 20971520 | tf_op jit(solution)/shard_map/bij,jbd->ibd/dot_general | solution.py:26
  267.9 12.4 %copy.55 = bf16[512,8,1024]{2,1,0:T(8,128)(2,1)} copy(bf16[512,8,1024]{0,2,1:T(8,128)(2,1)} %convert_bitcast_fusion.2) | data formatting | bytes 16777216 | tf_op jit(solution)/shard_map/convert_element_type | solution.py:28
  280.4 126.5 %all-to-all-done.2 = bf16[16,256,1024]{2,0,1:T(8,128)(2,1)} async-done(((bf16[16,256,1024]{2,0,1:T(8,128)(2,1)}), bf16[16,256,1024]{2,0,1:T(8,128)(2,1)}, u32[]{:S(2)}, u32[]{:S(2)}) %all-to-all-start.2) | async-done | bytes 8388640 | tf_op jit(solution)/shard_map/all_to_all | solution.py:35
  406.8 3.7 all-to-all-start.1
  410.6 15.8 %copy.59 = bf16[32,16,8,1024]{3,2,1,0:T(8,128)(2,1)} copy(bf16[32,16,8,1024]{3,1,2,0:T(8,128)(2,1)} %bitcast.12) | data formatting | bytes 16777216 | tf_op jit(solution)/shard_map/all_to_all | solution.py:35
  426.4 14.3 %convert_bitcast_fusion.1 = bf16[512,8,1024]{0,2,1:T(8,128)(2,1)} fusion(bf16[8,512,512]{2,1,0:T(8,128)(2,1)S(1)} %copy-done.2, bf16[512,8,1024]{2,1,0:T(8,128)(2,1)} %bitcast.51), kind=kOutput, calls=%fused_computation.25 | convolution fusion | flops 4299161600 | bytes 20971520 | tf_op jit(solution)/shard_map/bij,ibd->jbd/dot_general | solution.py:39
  440.7 12.6 %copy.61 = bf16[512,8,1024]{2,1,0:T(8,128)(2,1)} copy(bf16[512,8,1024]{0,2,1:T(8,128)(2,1)} %convert_bitcast_fusion.1) | data formatting | bytes 16777216 | tf_op jit(solution)/shard_map/convert_element_type | solution.py:41
  453.3 143.4 %all-to-all-done.1 = bf16[512,8,1024]{2,1,0:T(8,128)(2,1)} async-done(((bf16[512,8,1024]{2,1,0:T(8,128)(2,1)}), bf16[512,8,1024]{2,1,0:T(8,128)(2,1)}, u32[]{:S(2)}, u32[]{:S(2)}) %all-to-all-start.1) | async-done | bytes 8388640 | tf_op jit(solution)/shard_map/all_to_all | solution.py:25
  596.7 4.1 all-to-all-start.3
  600.8 30.9 %broadcast_multiply_fusion = f32[8,512,512]{2,1,0:T(8,128)} fusion(bf16[512,8,1024]{2,1,0:T(8,128)(2,1)} %bitcast.50, bf16[512,8,1024]{2,1,0:T(8,128)(2,1)} %bitcast.52), kind=kOutput, calls=%fused_computation.37 | convolution fusion | flops 4297064448 | bytes 25165824 | tf_op jit(solution)/shard_map/ibd,jbd->bij/dot_general | solution.py:48
  631.8 11.3 %convert_bitcast_fusion = f32[16,32,8,1024]{3,2,0,1:T(8,128)} fusion(bf16[32,16,8,1024]{3,2,1,0:T(8,128)(2,1)} %bitcast.20), kind=kLoop, calls=%fused_computation.20 | loop fusion | flops 4194304 | bytes 25165824 | tf_op jit(solution)/shard_map/convert_element_type | solution.py:54
  643.1 143.5 %all-to-all-done.3 = bf16[512,8,1024]{2,1,0:T(8,128)(2,1)} async-done(((bf16[512,8,1024]{2,1,0:T(8,128)(2,1)}), bf16[512,8,1024]{2,1,0:T(8,128)(2,1)}, u32[]{:S(2)}, u32[]{:S(2)}) %all-to-all-start.3) | async-done | bytes 8388640 | tf_op jit(solution)/shard_map/all_to_all | solution.py:38
  786.6 18.8 %fusion.8 = bf16[16,256,1024]{2,1,0:T(8,128)(2,1)} fusion(bf16[16,256,1024]{2,1,0:T(8,128)(2,1)} %bitcast.48, bf16[16,256,1024]{2,1,0:T(8,128)(2,1)} %bitcast.44, bf16[16,256,256]{2,1,0:T(8,128)(2,1)S(1)} %copy-done, bf16[16,32,8,1024]{3,2,0,1:T(8,128)(2,1)} %bitcast.16, bf16[32,16,8,1024]{3,2,1,0:T(8,128)(2,1)} %bitcast.20), kind=kOutput, calls=%fused_computation.15 | convolution fusion | flops 2206203904 | bytes 44040192 | tf_op jit(solution)/shard_map/apq,apd->aqd/dot_general | solution.py:58
  805.3 10.2 %broadcast_multiply_fusion.1 = f32[16,256,256]{2,1,0:T(8,128)} fusion(bf16[16,256,1024]{2,1,0:T(8,128)(2,1)} %bitcast.45, bf16[16,32,8,1024]{3,2,0,1:T(8,128)(2,1)} %bitcast.16), kind=kOutput, calls=%fused_computation.38 | convolution fusion | flops 2148532224 | bytes 20971520 | tf_op jit(solution)/shard_map/apd,aqd->apq/dot_general | solution.py:61
  815.5 7.0 copy.56
  822.5 9.8 %fusion.13 = bf16[1,4096,1024]{2,1,0:T(8,128)(2,1)} fusion(f32[1,4096,1024]{2,1,0:T(8,128)S(1)} %bitcast.46, bf16[1,4096,1024]{2,1,0:T(8,128)(2,1)} %param.4), kind=kLoop, calls=%fused_computation.21 | loop fusion | flops 29360128 | bytes 33554432 | tf_op jit(solution)/shard_map/convert_element_type | solution.py:55
  (6 shorter events, 1.6 us)
Async XLA Ops:
  0.6 1.6 copy-start
  22.8 194.0 %all-to-all-start = ((bf16[16,256,1024]{2,0,1:T(8,128)(2,1)}), bf16[16,256,1024]{2,0,1:T(8,128)(2,1)}, u32[]{:S(2)}, u32[]{:S(2)}) async-start(bf16[16,256,1024]{2,0,1:T(8,128)(2,1)} %copy.51), calls=%async_computation | async-start | bytes 16777216 | tf_op jit(solution)/shard_map/all_to_all | solution.py:22
  216.8 190.0 %all-to-all-start.2 = ((bf16[16,256,1024]{2,0,1:T(8,128)(2,1)}), bf16[16,256,1024]{2,0,1:T(8,128)(2,1)}, u32[]{:S(2)}, u32[]{:S(2)}) async-start(bf16[16,256,1024]{2,0,1:T(8,128)(2,1)} %copy.57), calls=%async_computation.2 | async-start | bytes 16777216 | tf_op jit(solution)/shard_map/all_to_all | solution.py:35
  220.7 16.0 %copy-start.1 = (bf16[8,512,512]{2,1,0:T(8,128)(2,1)S(1)}, bf16[8,512,512]{2,1,0:T(8,128)(2,1)}, u32[]{:S(2)}) copy-start(bf16[8,512,512]{2,1,0:T(8,128)(2,1)} %param.7) | copy-start | bytes 12582916
  406.8 189.9 %all-to-all-start.1 = ((bf16[512,8,1024]{2,1,0:T(8,128)(2,1)}), bf16[512,8,1024]{2,1,0:T(8,128)(2,1)}, u32[]{:S(2)}, u32[]{:S(2)}) async-start(bf16[512,8,1024]{2,1,0:T(8,128)(2,1)} %copy.55), calls=%async_computation.1 | async-start | bytes 16777216 | tf_op jit(solution)/shard_map/all_to_all | solution.py:25
  410.5 15.8 %copy-start.2 = (bf16[8,512,512]{2,1,0:T(8,128)(2,1)S(1)}, bf16[8,512,512]{2,1,0:T(8,128)(2,1)}, u32[]{:S(2)}) copy-start(bf16[8,512,512]{2,1,0:T(8,128)(2,1)} %param.7) | copy-start | bytes 12582916
  596.7 189.9 %all-to-all-start.3 = ((bf16[512,8,1024]{2,1,0:T(8,128)(2,1)}), bf16[512,8,1024]{2,1,0:T(8,128)(2,1)}, u32[]{:S(2)}, u32[]{:S(2)}) async-start(bf16[512,8,1024]{2,1,0:T(8,128)(2,1)} %copy.61), calls=%async_computation.3 | async-start | bytes 16777216 | tf_op jit(solution)/shard_map/all_to_all | solution.py:38
where the time goes:
time: 839 us; the launch traced here: 833 us
  waiting for transfers between devices  577 us (69%)
  matrix products  115 us (14%)
  local copies, waits for them, and re-layouts  88.2 us (11%)
  other arithmetic  32.5 us (4%)
  starting transfers between devices  19.6 us (2%)
    all_to_all x1, waiting for transfers between devices, shards(): lax.all_to_all(first, 'seq', split_axis=1, concat_axis=0, tiled=True)  163 us
    all_to_all x1, waiting for transfers between devices, shards(): lax.all_to_all(jnp.einsum('bij,ibd->jbd', right_factor, grad_cols, prefer...  144 us
    all_to_all x1, waiting for transfers between devices, shards(): lax.all_to_all(jnp.einsum('bij,jbd->ibd', right_factor, first_cols, prefe...  143 us
    all_to_all x1, waiting for transfers between devices, shards(): lax.all_to_all(grad_second, 'seq', split_axis=1, concat_axis=0, tiled=True)  126 us
    dot_general x1, matrix products, shards(): jnp.einsum('bij,jbd->ibd', right_factor, first_cols, preferred_element_ty...  31.2 us
    dot_general x1, matrix products, shards(): jnp.einsum('ibd,jbd->bij', grad_cols, first_cols, preferred_element_type=...  30.9 us
    dot_general x1, matrix products, shards(): jnp.einsum('apq,apd->aqd', left_factor, grad_first, preferred_element_typ...  18.8 us
  transfers between devices with their start and end apart: 4, of which 4 were waited for; matrix products, arithmetic and copies ran while one was open for 20% of the time, Pallas kernels for 0%

commit v1 on v0

--- a/solution.py
+++ b/solution.py
@@ -1,12 +1,16 @@
+import functools
+
 import jax
 import jax.numpy as jnp
 from jax import lax
+from jax.experimental import pallas as pl
+from jax.experimental.pallas import tpu as pltpu
 from jax.sharding import PartitionSpec as P
 
 grad_unscale = 1.0 / 32.0
 
 
-def shards(tokens, cotangent, left_factor, right_factor):
+def plain_shards(tokens, cotangent, left_factor, right_factor):
     a_rows = left_factor.shape[0]
     block_len = left_factor.shape[1]
     channels = tokens.shape[2]
@@ -63,6 +67,170 @@
     return (output.reshape(tokens.shape), tokens_grad.reshape(tokens.shape), left_grad, right_grad)
 
 
+def exchange(parts):
+    return lax.all_to_all(parts, "seq", split_axis=0, concat_axis=0, tiled=True)
+
+
+def after(value, *others):
+    return lax.optimization_barrier((value,) + others)[0]
+
+
+def call(kernel, n, in_specs, out_specs, out_shape, cost, aliases=None):
+    return pl.pallas_call(
+        kernel,
+        grid=(n,),
+        in_specs=in_specs,
+        out_specs=out_specs,
+        out_shape=out_shape,
+        input_output_aliases=aliases or {},
+        cost_estimate=pl.CostEstimate(flops=cost[0], bytes_accessed=cost[1], transcendentals=0),
+        compiler_params=pltpu.CompilerParams(vmem_limit_bytes=48 * 1024 * 1024),
+    )
+
+
+def row_spec(rows, columns, lo=0):
+    return pl.BlockSpec((1, rows, columns), lambda a: (a + lo, 0, 0))
+
+
+def split_spec(devices, b_rows, channels, lo=0):
+    return pl.BlockSpec((devices, 1, b_rows, channels), lambda a: (0, a + lo, 0, 0))
+
+
+def store_split(out_ref, value):
+    devices, _, b_rows, channels = out_ref.shape
+    out_ref[:, 0] = value.reshape(devices, b_rows, channels).astype(out_ref.dtype)
+
+
+def load_split(in_ref):
+    devices, _, b_rows, channels = in_ref.shape
+    return in_ref[:, 0].astype(jnp.float32).reshape(devices * b_rows, channels)
+
+
+def first_kernel(l_ref, x_ref, o_ref):
+    store_split(o_ref, jnp.dot(l_ref[0], x_ref[0], preferred_element_type=jnp.float32))
+
+
+def grad_second_kernel(x_ref, g_ref, o_ref):
+    x = x_ref[0].astype(jnp.float32)
+    store_split(o_ref, g_ref[0].astype(jnp.float32) * (x * jax.nn.sigmoid(x)))
+
+
+def output_kernel(x_ref, second_ref, o_ref):
+    x = x_ref[0].astype(jnp.float32)
+    o_ref[0] = (load_split(second_ref) * (x * jax.nn.sigmoid(x))).astype(o_ref.dtype)
+
+
+def last_kernel(l_ref, x_ref, g_ref, second_ref, grad_ref, *rest):
+    tokens_grad_ref, left_ref = rest[-2:]
+    x = x_ref[0].astype(jnp.float32)
+    s = jax.nn.sigmoid(x)
+    gate = g_ref[0].astype(jnp.float32) * load_split(second_ref) * s * (1.0 + x * (1.0 - s))
+    grad_first = load_split(grad_ref).astype(jnp.bfloat16)
+    back = lax.dot_general(
+        l_ref[0], grad_first, (((0,), (0,)), ((), ())), preferred_element_type=jnp.float32
+    )
+    tokens_grad_ref[0] = (back + gate).astype(tokens_grad_ref.dtype)
+    left_term = lax.dot_general(
+        grad_first, x_ref[0], (((1,), (1,)), ((), ())), preferred_element_type=jnp.float32
+    )
+    left_ref[0] = left_term * grad_unscale
+
+
+def shards(tokens, cotangent, left_factor, right_factor):
+    a_rows, block_len, _ = left_factor.shape
+    b_rows = right_factor.shape[0]
+    channels = tokens.shape[2]
+    devices = block_len // b_rows
+    if b_rows % 8 or a_rows % 4 or tokens.shape[0] != 1:
+        return plain_shards(tokens, cotangent, left_factor, right_factor)
+    head = a_rows // 4
+    tail = a_rows - head
+    x = tokens.reshape(a_rows, block_len, channels)
+    g = cotangent.reshape(a_rows, block_len, channels)
+    row_bytes = block_len * channels * 2
+    row_flops = 2 * block_len * block_len * channels
+    row = functools.partial(row_spec, block_len, channels)
+    square = functools.partial(row_spec, block_len, block_len)
+    split = functools.partial(split_spec, devices, b_rows, channels)
+
+    def split_shape(n):
+        return jax.ShapeDtypeStruct((devices, n, b_rows, channels), jnp.bfloat16)
+
+    def first_part(lo, n):
+        return call(
+            first_kernel,
+            n,
+            [square(lo), row(lo)],
+            split(),
+            split_shape(n),
+            (n * row_flops, 2 * n * row_bytes),
+        )(left_factor, x)
+
+    first_0 = exchange(first_part(0, head))
+    first_1 = exchange(after(first_part(head, tail), first_0))
+    grad_second = call(
+        grad_second_kernel,
+        a_rows,
+        [row(), row()],
+        split(),
+        split_shape(a_rows),
+        (a_rows * row_bytes * 5, 3 * a_rows * row_bytes),
+    )(x, g)
+    grad_cols = exchange(after(grad_second, first_0)).reshape(devices * a_rows, b_rows, channels)
+    first_cols = jnp.concatenate([first_0, first_1], axis=1).reshape(
+        devices * a_rows, b_rows, channels
+    )
+    second_cols = jnp.einsum(
+        "bij,jbd->ibd", right_factor, first_cols, preferred_element_type=jnp.float32
+    ).astype(jnp.bfloat16)
+    second = exchange(second_cols.reshape(devices, a_rows, b_rows, channels))
+    grad_rows = (
+        jnp.einsum("bij,ibd->jbd", right_factor, grad_cols, preferred_element_type=jnp.float32)
+        .astype(jnp.bfloat16)
+        .reshape(devices, a_rows, b_rows, channels)
+    )
+    grad_first_0 = exchange(grad_rows[:, :tail])
+    right_term = jnp.einsum(
+        "ibd,jbd->bij", grad_cols, first_cols, preferred_element_type=jnp.float32
+    )
+    right_grad = (
+        lax.psum_scatter(right_term, "batch", scatter_dimension=1, tiled=True) * grad_unscale
+    )
+    output = call(
+        output_kernel,
+        a_rows,
+        [row(), split()],
+        row(),
+        jax.ShapeDtypeStruct(x.shape, jnp.bfloat16),
+        (a_rows * row_bytes * 5, 3 * a_rows * row_bytes),
+    )(x, second)
+    grad_first_0, output, right_grad = lax.optimization_barrier(
+        (grad_first_0, output, right_grad)
+    )
+    grad_first_1 = exchange(after(grad_rows[:, tail:], grad_first_0))
+
+    def last_part(lo, n, grad_first, *held):
+        return call(
+            last_kernel,
+            n,
+            [square(lo), row(lo), row(lo), split(lo), split()]
+            + [pl.BlockSpec(memory_space=pl.ANY)] * len(held),
+            (row(lo), square(lo)),
+            (
+                jax.ShapeDtypeStruct(x.shape, jnp.bfloat16),
+                jax.ShapeDtypeStruct(left_factor.shape, jnp.float32),
+            ),
+            (2 * n * row_flops, 5 * n * row_bytes),
+            {5 + k: k for k in range(len(held))},
+        )(left_factor, x, g, second, grad_first, *held)
+
+    held = last_part(0, tail, grad_first_0)
+    grad_first_1, *held = lax.optimization_barrier((grad_first_1, *held))
+    tokens_grad, left_term = last_part(tail, head, grad_first_1, *held)
+    left_grad = lax.psum_scatter(left_term, "batch", scatter_dimension=1, tiled=True)
+    return (output.reshape(tokens.shape), tokens_grad.reshape(tokens.shape), left_grad, right_grad)
+
+
 def solution(mesh):
     return jax.shard_map(
         shards,

time: 839 us -> 801 us (0.955)
  Pallas kernels: 0 us -> 67.7 us
  local copies, waits for them, and re-layouts: 88.2 us -> 35.9 us
  matrix products: 115 us -> 64.4 us
  other arithmetic: 32.5 us -> 7.54 us
  waiting for transfers between devices: 577 us -> 587 us
    pallas_call x0 -> x6, Pallas kernels: none -> 67.7 us  [the longest x2 23.9 us: last_part(): call(last_kernel, n, [square(lo), row(lo), row(lo), split(lo), split()] +...]
    dot_general x3 -> x0, matrix products: 38.1 us -> none  [the longest x1 18.8 us: shards(): jnp.einsum('apq,apd->aqd', left_factor, grad_first, preferred_element_typ...]
    convert_element_type x3 -> x0, other arithmetic: 32.5 us -> none  [the longest x1 11.4 us: shards(): grad_second = (upstream * silu_x).astype(jnp.bfloat16)]
    all_to_all x2 -> x0, local copies, waits for them, and re-layouts: 31.8 us -> none  [the longest x1 16 us: shards(): lax.all_to_all(first, 'seq', split_axis=1, concat_axis=0, tiled=True)]
    convert_element_type x5 -> x2, local copies, waits for them, and re-layouts: 54.8 us -> 23.1 us  [the longest x1 11.8 us: shards(): second_cols = jnp.einsum('bij,jbd->ibd', right_factor, first_cols, prefer...]
    dot_general x1, matrix products: 31.2 us -> 18.6 us  [shards(): jnp.einsum('bij,jbd->ibd', right_factor, first_cols, preferred_element_ty...]
    all_to_all x4 -> x6, waiting for transfers between devices: 577 us -> 587 us  [exchange(): return lax.all_to_all(parts, 'seq', split_axis=0, concat_axis=0, tiled=True)]
    slice x0 -> x2, local copies, waits for them, and re-layouts: none -> 9.84 us  [the longest x1 6.65 us: shards(): grad_first_0 = exchange(grad_rows[:, :tail])]
  transfers between devices with their start and end apart: 4 -> 6, of which waited for: 4 -> 6; matrix products, arithmetic and copies ran while one was open for 20% -> 13% of each run, Pallas kernels for 0% -> 7%
where the time goes in v1:
time: 801 us; the launch traced here: 790 us
  waiting for transfers between devices  587 us (73%)
  Pallas kernels  67.7 us (8%)
  matrix products  64.4 us (8%)
  local copies, waits for them, and re-layouts  35.9 us (4%)
  starting transfers between devices  26.2 us (3%)
    all_to_all x6, waiting for transfers between devices, exchange(): return lax.all_to_all(parts, 'seq', split_axis=0, concat_axis=0, tiled=True)  587 us
    dot_general x1, matrix products, shards(): jnp.einsum('ibd,jbd->bij', grad_cols, first_cols, preferred_element_type=...  31 us
    all_to_all x6, starting transfers between devices, exchange(): return lax.all_to_all(parts, 'seq', split_axis=0, concat_axis=0, tiled=True)  26.2 us
    pallas_call x2, Pallas kernels, last_part(): call(last_kernel, n, [square(lo), row(lo), row(lo), split(lo), split()] +...  23.9 us
    dot_general x1, matrix products, shards(): jnp.einsum('bij,jbd->ibd', right_factor, first_cols, preferred_element_ty...  18.6 us
  transfers between devices with their start and end apart: 6, of which 6 were waited for; matrix products, arithmetic and copies ran while one was open for 13% of the time, Pallas kernels for 7%

profile of v1, /device:TPU:0, one launch (start us, length us, event | category | flops | bytes accessed | tf_op | source)
XLA Modules:
  0.0 789.6 jit_solution(15578611449659756956)
XLA Ops:
  6.8 7.4 all-to-all-start
  14.3 10.7 %shard_map.77 = bf16[32,12,8,1024]{3,2,1,0:T(8,128)(2,1)} custom-call(bf16[16,256,256]{2,1,0:T(8,128)(2,1)S(1)} %copy-done.1, bf16[16,256,1024]{2,1,0:T(8,128)(2,1)} %bitcast.15), custom_call_target="tpu_custom_call" | custom-call | flops 1610612736 | bytes 12582912 | tf_op jit(solution)/shard_map/pallas_call | solution.py:160
  24.9 38.2 %all-to-all-done = bf16[32,4,8,1024]{3,2,1,0:T(8,128)(2,1)} async-done(((bf16[32,4,8,1024]{3,2,1,0:T(8,128)(2,1)}), bf16[32,4,8,1024]{3,2,1,0:T(8,128)(2,1)}, u32[]{:S(2)}, u32[]{:S(2)}) %all-to-all-start) | async-done | bytes 2097184 | tf_op jit(solution)/shard_map/all_to_all | solution.py:71
  63.1 4.1 all-to-all-start.3
  67.3 14.9 %shard_map.75 = bf16[32,16,8,1024]{3,2,1,0:T(8,128)(2,1)} custom-call(bf16[16,256,1024]{2,1,0:T(8,128)(2,1)} %bitcast.16, bf16[16,256,1024]{2,1,0:T(8,128)(2,1)} %bitcast.20), custom_call_target="tpu_custom_call" | custom-call | flops 41943040 | bytes 25165824 | tf_op jit(solution)/shard_map/pallas_call | solution.py:171
  82.2 125.1 %all-to-all-done.3 = bf16[32,12,8,1024]{3,2,1,0:T(8,128)(2,1)} async-done(((bf16[32,12,8,1024]{3,2,1,0:T(8,128)(2,1)}), bf16[32,12,8,1024]{3,2,1,0:T(8,128)(2,1)}, u32[]{:S(2)}, u32[]{:S(2)}) %all-to-all-start.3) | async-done | bytes 6291488 | tf_op jit(solution)/shard_map/all_to_all | solution.py:71
  207.3 3.7 all-to-all-start.1
  211.0 7.5 pad_maximum_fusion
  218.5 18.6 %convert_bitcast_fusion = bf16[512,8,1024]{2,0,1:T(8,128)(2,1)} fusion(bf16[8,512,512]{2,1,0:T(8,128)(2,1)} %param.7, bf16[512,8,1024]{2,1,0:T(8,128)(2,1)} %bitcast.28), kind=kOutput, calls=%fused_computation.1 | convolution fusion | flops 4299161600 | bytes 20971520 | tf_op jit(solution)/shard_map/bij,jbd->ibd/dot_general | solution.py:183
  237.2 11.8 %copy.14 = bf16[512,8,1024]{2,1,0:T(8,128)(2,1)} copy(bf16[512,8,1024]{2,0,1:T(8,128)(2,1)} %convert_bitcast_fusion) | data formatting | bytes 16777216 | tf_op jit(solution)/shard_map/convert_element_type | solution.py:185
  249.0 148.1 %all-to-all-done.1 = bf16[32,16,8,1024]{3,2,1,0:T(8,128)(2,1)} async-done(((bf16[32,16,8,1024]{3,2,1,0:T(8,128)(2,1)}), bf16[32,16,8,1024]{3,2,1,0:T(8,128)(2,1)}, u32[]{:S(2)}, u32[]{:S(2)}) %all-to-all-start.1) | async-done | bytes 8388640 | tf_op jit(solution)/shard_map/all_to_all | solution.py:71
  397.1 3.7 all-to-all-start.4
  400.8 14.8 %convert_bitcast_fusion.1 = bf16[512,8,1024]{2,0,1:T(8,128)(2,1)} fusion(bf16[8,512,512]{2,1,0:T(8,128)(2,1)} %param.7, bf16[512,8,1024]{2,1,0:T(8,128)(2,1)} %bitcast.2), kind=kOutput, calls=%fused_computation.2 | convolution fusion | flops 4299161600 | bytes 20971520 | tf_op jit(solution)/shard_map/bij,ibd->jbd/dot_general | solution.py:188
  415.6 11.3 %copy.12 = bf16[512,8,1024]{2,1,0:T(8,128)(2,1)} copy(bf16[512,8,1024]{2,0,1:T(8,128)(2,1)} %convert_bitcast_fusion.1) | data formatting | bytes 16777216 | tf_op jit(solution)/shard_map/convert_element_type | solution.py:189
  427.0 6.7 slice.8
  433.6 153.4 %all-to-all-done.4.second_ref = bf16[32,16,8,1024]{3,2,1,0:T(8,128)(2,1)} async-done(((bf16[32,16,8,1024]{3,2,1,0:T(8,128)(2,1)}), bf16[32,16,8,1024]{3,2,1,0:T(8,128)(2,1)}, u32[]{:S(2)}, u32[]{:S(2)}) %all-to-all-start.4) | async-done | bytes 8388640 | tf_op jit(solution)/shard_map/all_to_all | solution.py:71
  587.0 3.8 all-to-all-start.2
  594.0 31.0 %broadcast_multiply_fusion = f32[8,512,512]{2,1,0:T(8,128)} fusion(bf16[512,8,1024]{2,1,0:T(8,128)(2,1)} %bitcast.29, bf16[512,8,1024]{2,1,0:T(8,128)(2,1)} %bitcast.2), kind=kOutput, calls=%fused_computation.10 | convolution fusion | flops 4297064448 | bytes 25165824 | tf_op jit(solution)/shard_map/ibd,jbd->bij/dot_general | solution.py:193
  624.9 14.9 %shard_map.78 = bf16[16,256,1024]{2,1,0:T(8,128)(2,1)} custom-call(bf16[16,256,1024]{2,1,0:T(8,128)(2,1)} %bitcast.17, bf16[32,16,8,1024]{3,2,1,0:T(8,128)(2,1)} %all-to-all-done.4.second_ref), custom_call_target="tpu_custom_call" | custom-call | flops 41943040 | bytes 25165824 | tf_op jit(solution)/shard_map/pallas_call | solution.py:199
  639.8 90.7 %all-to-all-done.2.grad_ref = bf16[32,12,8,1024]{3,2,1,0:T(8,128)(2,1)} async-done(((bf16[32,12,8,1024]{3,2,1,0:T(8,128)(2,1)}), bf16[32,12,8,1024]{3,2,1,0:T(8,128)(2,1)}, u32[]{:S(2)}, u32[]{:S(2)}) %all-to-all-start.2) | async-done | bytes 6291488 | tf_op jit(solution)/shard_map/all_to_all | solution.py:71
  730.5 3.5 all-to-all-start.5
  734.0 17.4 %shard_map.79 = (bf16[16,256,1024]{2,1,0:T(8,128)(2,1)}, f32[16,256,256]{2,1,0:T(8,128)}) custom-call(bf16[16,256,256]{2,1,0:T(8,128)(2,1)S(1)} %copy-done.1, bf16[16,256,1024]{2,1,0:T(8,128)(2,1)} %bitcast.18, bf16[16,256,1024]{2,1,0:T(8,128)(2,1)} %bitcast.21, bf16[32,16,8,1024]{3,2,1,0:T(8,128)(2,1)} %all-to-all-done.4.second_ref, ...), custom_call_target="tpu_custom_call" | custom-call | flops 3221225472 | bytes 31457280 | tf_op jit(solution)/shard_map/pallas_call | solution.py:213
  751.5 31.5 %all-to-all-done.5.grad_ref = bf16[32,4,8,1024]{3,2,1,0:T(8,128)(2,1)} async-done(((bf16[32,4,8,1024]{3,2,1,0:T(8,128)(2,1)}), bf16[32,4,8,1024]{3,2,1,0:T(8,128)(2,1)}, u32[]{:S(2)}, u32[]{:S(2)}) %all-to-all-start.5) | async-done | bytes 2097184 | tf_op jit(solution)/shard_map/all_to_all | solution.py:71
  782.9 6.5 shard_map.80
  (8 shorter events, 9.4 us)
Async XLA Ops:
  0.6 1.6 copy-start
  2.2 12.0 %copy-start.1 = (bf16[16,256,256]{2,1,0:T(8,128)(2,1)S(1)}, bf16[16,256,256]{2,1,0:T(8,128)(2,1)}, u32[]{:S(2)}) copy-start(bf16[16,256,256]{2,1,0:T(8,128)(2,1)} %l_ref.7) | copy-start | bytes 6291460
  5.5 1.3 copy-start.2
  6.8 56.3 %all-to-all-start = ((bf16[32,4,8,1024]{3,2,1,0:T(8,128)(2,1)}), bf16[32,4,8,1024]{3,2,1,0:T(8,128)(2,1)}, u32[]{:S(2)}, u32[]{:S(2)}) async-start(bf16[32,4,8,1024]{3,2,1,0:T(8,128)(2,1)} %copy-done.2), calls=%async_computation | async-start | bytes 4194304 | tf_op jit(solution)/shard_map/all_to_all | solution.py:71
  63.1 144.2 %all-to-all-start.3 = ((bf16[32,12,8,1024]{3,2,1,0:T(8,128)(2,1)}), bf16[32,12,8,1024]{3,2,1,0:T(8,128)(2,1)}, u32[]{:S(2)}, u32[]{:S(2)}) async-start(bf16[32,12,8,1024]{3,2,1,0:T(8,128)(2,1)} %shard_map.77), calls=%async_computation.3 | async-start | bytes 12582912 | tf_op jit(solution)/shard_map/all_to_all | solution.py:71
  207.3 189.8 %all-to-all-start.1 = ((bf16[32,16,8,1024]{3,2,1,0:T(8,128)(2,1)}), bf16[32,16,8,1024]{3,2,1,0:T(8,128)(2,1)}, u32[]{:S(2)}, u32[]{:S(2)}) async-start(bf16[32,16,8,1024]{3,2,1,0:T(8,128)(2,1)} %shard_map.75), calls=%async_computation.1 | async-start | bytes 16777216 | tf_op jit(solution)/shard_map/all_to_all | solution.py:71
  397.1 189.8 %all-to-all-start.4 = ((bf16[32,16,8,1024]{3,2,1,0:T(8,128)(2,1)}), bf16[32,16,8,1024]{3,2,1,0:T(8,128)(2,1)}, u32[]{:S(2)}, u32[]{:S(2)}) async-start(bf16[32,16,8,1024]{3,2,1,0:T(8,128)(2,1)} %bitcast.23), calls=%async_computation.4 | async-start | bytes 16777216 | tf_op jit(solution)/shard_map/all_to_all | solution.py:71
  587.0 143.6 %all-to-all-start.2 = ((bf16[32,12,8,1024]{3,2,1,0:T(8,128)(2,1)}), bf16[32,12,8,1024]{3,2,1,0:T(8,128)(2,1)}, u32[]{:S(2)}, u32[]{:S(2)}) async-start(bf16[32,12,8,1024]{3,2,1,0:T(8,128)(2,1)} %slice.8), calls=%async_computation.2 | async-start | bytes 12582912 | tf_op jit(solution)/shard_map/all_to_all | solution.py:71
  730.5 52.4 %all-to-all-start.5 = ((bf16[32,4,8,1024]{3,2,1,0:T(8,128)(2,1)}), bf16[32,4,8,1024]{3,2,1,0:T(8,128)(2,1)}, u32[]{:S(2)}, u32[]{:S(2)}) async-start(bf16[32,4,8,1024]{3,2,1,0:T(8,128)(2,1)} %slice.9), calls=%async_computation.5 | async-start | bytes 4194304 | tf_op jit(solution)/shard_map/all_to_all | solution.py:71

commit v2 on v1

--- a/solution.py
+++ b/solution.py
@@ -75,7 +75,7 @@
     return lax.optimization_barrier((value,) + others)[0]
 
 
-def call(kernel, n, in_specs, out_specs, out_shape, cost, aliases=None):
+def call(kernel, n, in_specs, out_specs, out_shape, cost, aliases=None, vmem_mib=48):
     return pl.pallas_call(
         kernel,
         grid=(n,),
@@ -84,7 +84,7 @@
         out_shape=out_shape,
         input_output_aliases=aliases or {},
         cost_estimate=pl.CostEstimate(flops=cost[0], bytes_accessed=cost[1], transcendentals=0),
-        compiler_params=pltpu.CompilerParams(vmem_limit_bytes=48 * 1024 * 1024),
+        compiler_params=pltpu.CompilerParams(vmem_limit_bytes=vmem_mib * 1024 * 1024),
     )
 
 
@@ -141,9 +141,9 @@
     b_rows = right_factor.shape[0]
     channels = tokens.shape[2]
     devices = block_len // b_rows
-    if b_rows % 8 or a_rows % 4 or tokens.shape[0] != 1:
+    if b_rows % 8 or a_rows % 8 or tokens.shape[0] != 1:
         return plain_shards(tokens, cotangent, left_factor, right_factor)
-    head = a_rows // 4
+    head = a_rows // 8
     tail = a_rows - head
     x = tokens.reshape(a_rows, block_len, channels)
     g = cotangent.reshape(a_rows, block_len, channels)
@@ -156,7 +156,7 @@
     def split_shape(n):
         return jax.ShapeDtypeStruct((devices, n, b_rows, channels), jnp.bfloat16)
 
-    def first_part(lo, n):
+    def first_part(lo, n, vmem_mib):
         return call(
             first_kernel,
             n,
@@ -164,10 +164,11 @@
             split(),
             split_shape(n),
             (n * row_flops, 2 * n * row_bytes),
+            vmem_mib=vmem_mib,
         )(left_factor, x)
 
-    first_0 = exchange(first_part(0, head))
-    first_1 = exchange(after(first_part(head, tail), first_0))
+    first_0 = exchange(first_part(0, head, 60))
+    first_1 = exchange(after(first_part(head, tail, 48), first_0))
     grad_second = call(
         grad_second_kernel,
         a_rows,

time: 801 us -> 794 us (level)
  transfers between devices with their start and end apart: 6 -> 6, of which waited for: 6 -> 6; matrix products, arithmetic and copies ran while one was open for 13% -> 13% of each run, Pallas kernels for 7% -> 8%
where the time goes in v2:
time: 794 us; the launch traced here: 783 us
  waiting for transfers between devices  584 us (74%)
  Pallas kernels  68.5 us (9%)
  matrix products  64.4 us (8%)
  local copies, waits for them, and re-layouts  32.9 us (4%)
  starting transfers between devices  24.9 us (3%)
    all_to_all x6, waiting for transfers between devices, exchange(): return lax.all_to_all(parts, 'seq', split_axis=0, concat_axis=0, tiled=True)  584 us
    dot_general x1, matrix products, shards(): jnp.einsum('ibd,jbd->bij', grad_cols, first_cols, preferred_element_type=...  31 us
    all_to_all x6, starting transfers between devices, exchange(): return lax.all_to_all(parts, 'seq', split_axis=0, concat_axis=0, tiled=True)  24.9 us
    pallas_call x2, Pallas kernels, last_part(): call(last_kernel, n, [square(lo), row(lo), row(lo), split(lo), split()] +...  23.7 us
    dot_general x1, matrix products, shards(): jnp.einsum('bij,jbd->ibd', right_factor, first_cols, preferred_element_ty...  18.7 us
  transfers between devices with their start and end apart: 6, of which 6 were waited for; matrix products, arithmetic and copies ran while one was open for 13% of the time, Pallas kernels for 8%

profile of v2, /device:TPU:0, one launch (start us, length us, event | category | flops | bytes accessed | tf_op | source)
XLA Modules:
  0.0 782.8 jit_solution(12666296929646019472)
XLA Ops:
  0.6 2.7 shard_map.76
  3.3 7.3 all-to-all-start
  10.6 12.3 %shard_map.77 = bf16[32,14,8,1024]{3,2,1,0:T(8,128)(2,1)} custom-call(bf16[16,256,256]{2,1,0:T(8,128)(2,1)S(1)} %copy-done, bf16[16,256,1024]{2,1,0:T(8,128)(2,1)} %bitcast.15), custom_call_target="tpu_custom_call" | custom-call | flops 1879048192 | bytes 14680064 | tf_op jit(solution)/shard_map/pallas_call | solution.py:160
  22.9 14.0 %all-to-all-done = bf16[32,2,8,1024]{3,2,1,0:T(8,128)(2,1)S(1)} async-done(((bf16[32,2,8,1024]{3,2,1,0:T(8,128)(2,1)}), bf16[32,2,8,1024]{3,2,1,0:T(8,128)(2,1)S(1)}, u32[]{:S(2)}, u32[]{:S(2)}) %all-to-all-start) | async-done | bytes 1048608 | tf_op jit(solution)/shard_map/all_to_all | solution.py:71
  36.9 3.7 all-to-all-start.3
  40.6 15.0 %shard_map.75 = bf16[32,16,8,1024]{3,2,1,0:T(8,128)(2,1)} custom-call(bf16[16,256,1024]{2,1,0:T(8,128)(2,1)} %bitcast.16, bf16[16,256,1024]{2,1,0:T(8,128)(2,1)} %bitcast.20), custom_call_target="tpu_custom_call" | custom-call | flops 41943040 | bytes 25165824 | tf_op jit(solution)/shard_map/pallas_call | solution.py:172
  55.6 148.1 %all-to-all-done.3 = bf16[32,14,8,1024]{3,2,1,0:T(8,128)(2,1)} async-done(((bf16[32,14,8,1024]{3,2,1,0:T(8,128)(2,1)}), bf16[32,14,8,1024]{3,2,1,0:T(8,128)(2,1)}, u32[]{:S(2)}, u32[]{:S(2)}) %all-to-all-start.3) | async-done | bytes 7340064 | tf_op jit(solution)/shard_map/all_to_all | solution.py:71
  203.7 3.7 all-to-all-start.1
  207.4 7.2 pad_maximum_fusion
  214.6 18.7 %convert_bitcast_fusion = bf16[512,8,1024]{2,0,1:T(8,128)(2,1)} fusion(bf16[8,512,512]{2,1,0:T(8,128)(2,1)} %param.7, bf16[512,8,1024]{2,1,0:T(8,128)(2,1)} %bitcast.28), kind=kOutput, calls=%fused_computation.1 | convolution fusion | flops 4299161600 | bytes 20971520 | tf_op jit(solution)/shard_map/bij,jbd->ibd/dot_general | solution.py:184
  233.3 11.8 %copy.14 = bf16[512,8,1024]{2,1,0:T(8,128)(2,1)} copy(bf16[512,8,1024]{2,0,1:T(8,128)(2,1)} %convert_bitcast_fusion) | data formatting | bytes 16777216 | tf_op jit(solution)/shard_map/convert_element_type | solution.py:186
  245.1 148.5 %all-to-all-done.1 = bf16[32,16,8,1024]{3,2,1,0:T(8,128)(2,1)} async-done(((bf16[32,16,8,1024]{3,2,1,0:T(8,128)(2,1)}), bf16[32,16,8,1024]{3,2,1,0:T(8,128)(2,1)}, u32[]{:S(2)}, u32[]{:S(2)}) %all-to-all-start.1) | async-done | bytes 8388640 | tf_op jit(solution)/shard_map/all_to_all | solution.py:71
  393.6 3.7 all-to-all-start.4
  397.3 14.8 %convert_bitcast_fusion.1 = bf16[512,8,1024]{2,0,1:T(8,128)(2,1)} fusion(bf16[8,512,512]{2,1,0:T(8,128)(2,1)} %param.7, bf16[512,8,1024]{2,1,0:T(8,128)(2,1)} %bitcast.2), kind=kOutput, calls=%fused_computation.2 | convolution fusion | flops 4299161600 | bytes 20971520 | tf_op jit(solution)/shard_map/bij,ibd->jbd/dot_general | solution.py:189
  412.1 11.3 %copy.12 = bf16[512,8,1024]{2,1,0:T(8,128)(2,1)} copy(bf16[512,8,1024]{2,0,1:T(8,128)(2,1)} %convert_bitcast_fusion.1) | data formatting | bytes 16777216 | tf_op jit(solution)/shard_map/convert_element_type | solution.py:190
  423.4 7.4 slice.8
  430.8 152.6 %all-to-all-done.4.second_ref = bf16[32,16,8,1024]{3,2,1,0:T(8,128)(2,1)} async-done(((bf16[32,16,8,1024]{3,2,1,0:T(8,128)(2,1)}), bf16[32,16,8,1024]{3,2,1,0:T(8,128)(2,1)}, u32[]{:S(2)}, u32[]{:S(2)}) %all-to-all-start.4) | async-done | bytes 8388640 | tf_op jit(solution)/shard_map/all_to_all | solution.py:71
  583.4 3.8 all-to-all-start.2
  589.6 31.0 %broadcast_multiply_fusion = f32[8,512,512]{2,1,0:T(8,128)} fusion(bf16[512,8,1024]{2,1,0:T(8,128)(2,1)} %bitcast.29, bf16[512,8,1024]{2,1,0:T(8,128)(2,1)} %bitcast.2), kind=kOutput, calls=%fused_computation.10 | convolution fusion | flops 4297064448 | bytes 25165824 | tf_op jit(solution)/shard_map/ibd,jbd->bij/dot_general | solution.py:194
  620.6 14.9 %shard_map.78 = bf16[16,256,1024]{2,1,0:T(8,128)(2,1)} custom-call(bf16[16,256,1024]{2,1,0:T(8,128)(2,1)} %bitcast.17, bf16[32,16,8,1024]{3,2,1,0:T(8,128)(2,1)} %all-to-all-done.4.second_ref), custom_call_target="tpu_custom_call" | custom-call | flops 41943040 | bytes 25165824 | tf_op jit(solution)/shard_map/pallas_call | solution.py:200
  635.5 114.8 %all-to-all-done.2.grad_ref = bf16[32,14,8,1024]{3,2,1,0:T(8,128)(2,1)} async-done(((bf16[32,14,8,1024]{3,2,1,0:T(8,128)(2,1)}), bf16[32,14,8,1024]{3,2,1,0:T(8,128)(2,1)}, u32[]{:S(2)}, u32[]{:S(2)}) %all-to-all-start.2) | async-done | bytes 7340064 | tf_op jit(solution)/shard_map/all_to_all | solution.py:71
  752.9 20.2 %shard_map.79 = (bf16[16,256,1024]{2,1,0:T(8,128)(2,1)}, f32[16,256,256]{2,1,0:T(8,128)}) custom-call(bf16[16,256,256]{2,1,0:T(8,128)(2,1)S(1)} %copy-done, bf16[16,256,1024]{2,1,0:T(8,128)(2,1)} %bitcast.18, bf16[16,256,1024]{2,1,0:T(8,128)(2,1)} %bitcast.21, bf16[32,16,8,1024]{3,2,1,0:T(8,128)(2,1)} %all-to-all-done.4.second_ref, ...), custom_call_target="tpu_custom_call" | custom-call | flops 3758096384 | bytes 36700160 | tf_op jit(solution)/shard_map/pallas_call | solution.py:214
  773.0 6.0 all-to-all-done.5.grad_ref
  779.1 3.5 shard_map.80
  (4 shorter events, 5.0 us)
Async XLA Ops:
  0.6 10.0 %copy-start = (bf16[16,256,256]{2,1,0:T(8,128)(2,1)S(1)}, bf16[16,256,256]{2,1,0:T(8,128)(2,1)}, u32[]{:S(2)}) copy-start(bf16[16,256,256]{2,1,0:T(8,128)(2,1)} %l_ref.7) | copy-start | bytes 6291460
  3.3 33.5 %all-to-all-start = ((bf16[32,2,8,1024]{3,2,1,0:T(8,128)(2,1)}), bf16[32,2,8,1024]{3,2,1,0:T(8,128)(2,1)S(1)}, u32[]{:S(2)}, u32[]{:S(2)}) async-start(bf16[32,2,8,1024]{3,2,1,0:T(8,128)(2,1)} %shard_map.76), calls=%async_computation | async-start | bytes 2097152 | tf_op jit(solution)/shard_map/all_to_all | solution.py:71
  36.9 166.8 %all-to-all-start.3 = ((bf16[32,14,8,1024]{3,2,1,0:T(8,128)(2,1)}), bf16[32,14,8,1024]{3,2,1,0:T(8,128)(2,1)}, u32[]{:S(2)}, u32[]{:S(2)}) async-start(bf16[32,14,8,1024]{3,2,1,0:T(8,128)(2,1)} %shard_map.77), calls=%async_computation.3 | async-start | bytes 14680064 | tf_op jit(solution)/shard_map/all_to_all | solution.py:71
  203.7 189.9 %all-to-all-start.1 = ((bf16[32,16,8,1024]{3,2,1,0:T(8,128)(2,1)}), bf16[32,16,8,1024]{3,2,1,0:T(8,128)(2,1)}, u32[]{:S(2)}, u32[]{:S(2)}) async-start(bf16[32,16,8,1024]{3,2,1,0:T(8,128)(2,1)} %shard_map.75), calls=%async_computation.1 | async-start | bytes 16777216 | tf_op jit(solution)/shard_map/all_to_all | solution.py:71
  393.6 189.8 %all-to-all-start.4 = ((bf16[32,16,8,1024]{3,2,1,0:T(8,128)(2,1)}), bf16[32,16,8,1024]{3,2,1,0:T(8,128)(2,1)}, u32[]{:S(2)}, u32[]{:S(2)}) async-start(bf16[32,16,8,1024]{3,2,1,0:T(8,128)(2,1)} %bitcast.25), calls=%async_computation.4 | async-start | bytes 16777216 | tf_op jit(solution)/shard_map/all_to_all | solution.py:71
  583.4 166.8 %all-to-all-start.2 = ((bf16[32,14,8,1024]{3,2,1,0:T(8,128)(2,1)}), bf16[32,14,8,1024]{3,2,1,0:T(8,128)(2,1)}, u32[]{:S(2)}, u32[]{:S(2)}) async-start(bf16[32,14,8,1024]{3,2,1,0:T(8,128)(2,1)} %slice.8), calls=%async_computation.2 | async-start | bytes 14680064 | tf_op jit(solution)/shard_map/all_to_all | solution.py:71
  750.2 28.9 %all-to-all-start.5 = ((bf16[32,2,8,1024]{3,2,1,0:T(8,128)(2,1)}), bf16[32,2,8,1024]{3,2,1,0:T(8,128)(2,1)S(1)}, u32[]{:S(2)}, u32[]{:S(2)}) async-start(bf16[32,2,8,1024]{3,2,1,0:T(8,128)(2,1)} %slice.9), calls=%async_computation.5 | async-start | bytes 2097152 | tf_op jit(solution)/shard_map/all_to_all | solution.py:71

commit v3 on v2

--- a/solution.py
+++ b/solution.py
@@ -107,7 +107,10 @@
 
 
 def first_kernel(l_ref, x_ref, o_ref):
-    store_split(o_ref, jnp.dot(l_ref[0], x_ref[0], preferred_element_type=jnp.float32))
+    devices, rows, b_rows, channels = o_ref.shape
+    for k in range(rows):
+        first = jnp.dot(l_ref[k], x_ref[k], preferred_element_type=jnp.float32)
+        o_ref[:, k] = first.reshape(devices, b_rows, channels).astype(o_ref.dtype)
 
 
 def grad_second_kernel(x_ref, g_ref, o_ref):
@@ -145,6 +148,7 @@
         return plain_shards(tokens, cotangent, left_factor, right_factor)
     head = a_rows // 8
     tail = a_rows - head
+    step = a_rows // 2
     x = tokens.reshape(a_rows, block_len, channels)
     g = cotangent.reshape(a_rows, block_len, channels)
     row_bytes = block_len * channels * 2
@@ -156,19 +160,19 @@
     def split_shape(n):
         return jax.ShapeDtypeStruct((devices, n, b_rows, channels), jnp.bfloat16)
 
-    def first_part(lo, n, vmem_mib):
-        return call(
-            first_kernel,
-            n,
-            [square(lo), row(lo)],
-            split(),
-            split_shape(n),
-            (n * row_flops, 2 * n * row_bytes),
-            vmem_mib=vmem_mib,
-        )(left_factor, x)
-
-    first_0 = exchange(first_part(0, head, 60))
-    first_1 = exchange(after(first_part(head, tail, 48), first_0))
+    first = call(
+        first_kernel,
+        a_rows // step,
+        [
+            pl.BlockSpec((step, block_len, block_len), lambda a: (a, 0, 0)),
+            pl.BlockSpec((step, block_len, channels), lambda a: (a, 0, 0)),
+        ],
+        pl.BlockSpec((devices, step, b_rows, channels), lambda a: (0, a, 0, 0)),
+        split_shape(a_rows),
+        (a_rows * row_flops, 2 * a_rows * row_bytes),
+        vmem_mib=60,
+    )(left_factor, x)
+    first_cols = exchange(first).reshape(devices * a_rows, b_rows, channels)
     grad_second = call(
         grad_second_kernel,
         a_rows,
@@ -177,10 +181,7 @@
         split_shape(a_rows),
         (a_rows * row_bytes * 5, 3 * a_rows * row_bytes),
     )(x, g)
-    grad_cols = exchange(after(grad_second, first_0)).reshape(devices * a_rows, b_rows, channels)
-    first_cols = jnp.concatenate([first_0, first_1], axis=1).reshape(
-        devices * a_rows, b_rows, channels
-    )
+    grad_cols = exchange(grad_second).reshape(devices * a_rows, b_rows, channels)
     second_cols = jnp.einsum(
         "bij,jbd->ibd", right_factor, first_cols, preferred_element_type=jnp.float32
     ).astype(jnp.bfloat16)

time: 794 us -> 792 us (level)
  waiting for transfers between devices: 584 us -> 600 us
    all_to_all x6 -> x5, waiting for transfers between devices: 584 us -> 600 us  [exchange(): return lax.all_to_all(parts, 'seq', split_axis=0, concat_axis=0, tiled=True)]
    all_to_all x6 -> x5, starting transfers between devices: 24.9 us -> 21.3 us  [exchange(): return lax.all_to_all(parts, 'seq', split_axis=0, concat_axis=0, tiled=True)]
  transfers between devices with their start and end apart: 6 -> 5, of which waited for: 6 -> 5; matrix products, arithmetic and copies ran while one was open for 13% -> 12% of each run, Pallas kernels for 8% -> 6%
where the time goes in v3:
time: 792 us; the launch traced here: 781 us
  waiting for transfers between devices  600 us (76%)
  matrix products  64.4 us (8%)
  Pallas kernels  61 us (8%)
  local copies, waits for them, and re-layouts  33.1 us (4%)
  starting transfers between devices  21.3 us (3%)
    all_to_all x5, waiting for transfers between devices, exchange(): return lax.all_to_all(parts, 'seq', split_axis=0, concat_axis=0, tiled=True)  600 us
    dot_general x1, matrix products, shards(): jnp.einsum('ibd,jbd->bij', grad_cols, first_cols, preferred_element_type=...  31 us
    pallas_call x2, Pallas kernels, last_part(): call(last_kernel, n, [square(lo), row(lo), row(lo), split(lo), split()] +...  23.7 us
    all_to_all x5, starting transfers between devices, exchange(): return lax.all_to_all(parts, 'seq', split_axis=0, concat_axis=0, tiled=True)  21.3 us
    dot_general x1, matrix products, shards(): jnp.einsum('bij,jbd->ibd', right_factor, first_cols, preferred_element_ty...  18.6 us
  transfers between devices with their start and end apart: 5, of which 5 were waited for; matrix products, arithmetic and copies ran while one was open for 12% of the time, Pallas kernels for 6%

profile of v3, /device:TPU:0, one launch (start us, length us, event | category | flops | bytes accessed | tf_op | source)
XLA Modules:
  0.0 780.6 jit_solution(11920153473778209452)
XLA Ops:
  0.6 7.4 shard_map.76
  8.0 7.4 all-to-all-start.2
  15.4 14.9 %shard_map.75 = bf16[32,16,8,1024]{3,2,1,0:T(8,128)(2,1)} custom-call(bf16[16,256,1024]{2,1,0:T(8,128)(2,1)} %bitcast.15, bf16[16,256,1024]{2,1,0:T(8,128)(2,1)} %bitcast.19), custom_call_target="tpu_custom_call" | custom-call | flops 41943040 | bytes 25165824 | tf_op jit(solution)/shard_map/pallas_call | solution.py:176
  30.3 171.1 %all-to-all-done.2 = bf16[32,16,8,1024]{3,2,1,0:T(8,128)(2,1)} async-done(((bf16[32,16,8,1024]{3,2,1,0:T(8,128)(2,1)}), bf16[32,16,8,1024]{3,2,1,0:T(8,128)(2,1)}, u32[]{:S(2)}, u32[]{:S(2)}) %all-to-all-start.2) | async-done | bytes 8388640 | tf_op jit(solution)/shard_map/all_to_all | solution.py:71
  201.5 3.7 all-to-all-start
  205.2 18.6 %convert_bitcast_fusion = bf16[512,8,1024]{2,0,1:T(8,128)(2,1)} fusion(bf16[8,512,512]{2,1,0:T(8,128)(2,1)} %param.7, bf16[512,8,1024]{2,1,0:T(8,128)(2,1)} %bitcast.5), kind=kOutput, calls=%fused_computation | convolution fusion | flops 4299161600 | bytes 20971520 | tf_op jit(solution)/shard_map/bij,jbd->ibd/dot_general | solution.py:185
  223.8 11.8 %copy.14 = bf16[512,8,1024]{2,1,0:T(8,128)(2,1)} copy(bf16[512,8,1024]{2,0,1:T(8,128)(2,1)} %convert_bitcast_fusion) | data formatting | bytes 16777216 | tf_op jit(solution)/shard_map/convert_element_type | solution.py:187
  235.7 155.7 %all-to-all-done = bf16[32,16,8,1024]{3,2,1,0:T(8,128)(2,1)} async-done(((bf16[32,16,8,1024]{3,2,1,0:T(8,128)(2,1)}), bf16[32,16,8,1024]{3,2,1,0:T(8,128)(2,1)}, u32[]{:S(2)}, u32[]{:S(2)}) %all-to-all-start) | async-done | bytes 8388640 | tf_op jit(solution)/shard_map/all_to_all | solution.py:71
  391.3 3.7 all-to-all-start.3
  395.0 14.8 %convert_bitcast_fusion.1 = bf16[512,8,1024]{2,0,1:T(8,128)(2,1)} fusion(bf16[8,512,512]{2,1,0:T(8,128)(2,1)} %param.7, bf16[512,8,1024]{2,1,0:T(8,128)(2,1)} %bitcast.2), kind=kOutput, calls=%fused_computation.1 | convolution fusion | flops 4299161600 | bytes 20971520 | tf_op jit(solution)/shard_map/bij,ibd->jbd/dot_general | solution.py:190
  409.9 11.5 %copy.12 = bf16[512,8,1024]{2,1,0:T(8,128)(2,1)} copy(bf16[512,8,1024]{2,0,1:T(8,128)(2,1)} %convert_bitcast_fusion.1) | data formatting | bytes 16777216 | tf_op jit(solution)/shard_map/convert_element_type | solution.py:191
  421.3 7.4 slice.8
  428.7 152.4 %all-to-all-done.3.second_ref = bf16[32,16,8,1024]{3,2,1,0:T(8,128)(2,1)} async-done(((bf16[32,16,8,1024]{3,2,1,0:T(8,128)(2,1)}), bf16[32,16,8,1024]{3,2,1,0:T(8,128)(2,1)}, u32[]{:S(2)}, u32[]{:S(2)}) %all-to-all-start.3) | async-done | bytes 8388640 | tf_op jit(solution)/shard_map/all_to_all | solution.py:71
  581.2 3.8 all-to-all-start.1
  585.0 2.4 slice.9
  587.4 31.0 %broadcast_multiply_fusion = f32[8,512,512]{2,1,0:T(8,128)} fusion(bf16[512,8,1024]{2,1,0:T(8,128)(2,1)} %bitcast.5, bf16[512,8,1024]{2,1,0:T(8,128)(2,1)} %bitcast.2), kind=kOutput, calls=%fused_computation.9 | convolution fusion | flops 4297064448 | bytes 25165824 | tf_op jit(solution)/shard_map/ibd,jbd->bij/dot_general | solution.py:195
  618.3 0.0 copy-start
  618.3 15.0 %shard_map.77 = bf16[16,256,1024]{2,1,0:T(8,128)(2,1)} custom-call(bf16[16,256,1024]{2,1,0:T(8,128)(2,1)} %bitcast.16, bf16[32,16,8,1024]{3,2,1,0:T(8,128)(2,1)} %all-to-all-done.3.second_ref), custom_call_target="tpu_custom_call" | custom-call | flops 41943040 | bytes 25165824 | tf_op jit(solution)/shard_map/pallas_call | solution.py:201
  633.4 114.6 %all-to-all-done.1.grad_ref = bf16[32,14,8,1024]{3,2,1,0:T(8,128)(2,1)} async-done(((bf16[32,14,8,1024]{3,2,1,0:T(8,128)(2,1)}), bf16[32,14,8,1024]{3,2,1,0:T(8,128)(2,1)}, u32[]{:S(2)}, u32[]{:S(2)}) %all-to-all-start.1) | async-done | bytes 7340064 | tf_op jit(solution)/shard_map/all_to_all | solution.py:71
  748.0 2.6 all-to-all-start.4
  750.6 0.0 copy-done
  750.6 20.2 %shard_map.78 = (bf16[16,256,1024]{2,1,0:T(8,128)(2,1)}, f32[16,256,256]{2,1,0:T(8,128)}) custom-call(bf16[16,256,256]{2,1,0:T(8,128)(2,1)S(1)} %copy-done, bf16[16,256,1024]{2,1,0:T(8,128)(2,1)} %bitcast.17, bf16[16,256,1024]{2,1,0:T(8,128)(2,1)} %bitcast.20, bf16[32,16,8,1024]{3,2,1,0:T(8,128)(2,1)} %all-to-all-done.3.second_ref, ...), custom_call_target="tpu_custom_call" | custom-call | flops 3758096384 | bytes 36700160 | tf_op jit(solution)/shard_map/pallas_call | solution.py:215
  770.8 6.0 all-to-all-done.4.grad_ref
  776.9 3.5 shard_map.79
Async XLA Ops:
  8.0 193.5 %all-to-all-start.2 = ((bf16[32,16,8,1024]{3,2,1,0:T(8,128)(2,1)}), bf16[32,16,8,1024]{3,2,1,0:T(8,128)(2,1)}, u32[]{:S(2)}, u32[]{:S(2)}) async-start(bf16[32,16,8,1024]{3,2,1,0:T(8,128)(2,1)} %shard_map.76), calls=%async_computation.2 | async-start | bytes 16777216 | tf_op jit(solution)/shard_map/all_to_all | solution.py:71
  201.5 189.9 %all-to-all-start = ((bf16[32,16,8,1024]{3,2,1,0:T(8,128)(2,1)}), bf16[32,16,8,1024]{3,2,1,0:T(8,128)(2,1)}, u32[]{:S(2)}, u32[]{:S(2)}) async-start(bf16[32,16,8,1024]{3,2,1,0:T(8,128)(2,1)} %shard_map.75), calls=%async_computation | async-start | bytes 16777216 | tf_op jit(solution)/shard_map/all_to_all | solution.py:71
  391.3 189.8 %all-to-all-start.3 = ((bf16[32,16,8,1024]{3,2,1,0:T(8,128)(2,1)}), bf16[32,16,8,1024]{3,2,1,0:T(8,128)(2,1)}, u32[]{:S(2)}, u32[]{:S(2)}) async-start(bf16[32,16,8,1024]{3,2,1,0:T(8,128)(2,1)} %bitcast.24), calls=%async_computation.3 | async-start | bytes 16777216 | tf_op jit(solution)/shard_map/all_to_all | solution.py:71
  581.2 166.8 %all-to-all-start.1 = ((bf16[32,14,8,1024]{3,2,1,0:T(8,128)(2,1)}), bf16[32,14,8,1024]{3,2,1,0:T(8,128)(2,1)}, u32[]{:S(2)}, u32[]{:S(2)}) async-start(bf16[32,14,8,1024]{3,2,1,0:T(8,128)(2,1)} %slice.8), calls=%async_computation.1 | async-start | bytes 14680064 | tf_op jit(solution)/shard_map/all_to_all | solution.py:71
  618.3 132.3 %copy-start = (bf16[16,256,256]{2,1,0:T(8,128)(2,1)S(1)}, bf16[16,256,256]{2,1,0:T(8,128)(2,1)}, u32[]{:S(2)}) copy-start(bf16[16,256,256]{2,1,0:T(8,128)(2,1)} %l_ref.5) | copy-start | bytes 6291460
  748.0 28.9 %all-to-all-start.4 = ((bf16[32,2,8,1024]{3,2,1,0:T(8,128)(2,1)}), bf16[32,2,8,1024]{3,2,1,0:T(8,128)(2,1)S(1)}, u32[]{:S(2)}, u32[]{:S(2)}) async-start(bf16[32,2,8,1024]{3,2,1,0:T(8,128)(2,1)} %slice.9), calls=%async_computation.4 | async-start | bytes 2097152 | tf_op jit(solution)/shard_map/all_to_all | solution.py:71
